TPU v7x, 128 devices: a whole 4x4x4 slice. The times are simulated.
128 devices in a mesh: gossip: 8 (over x, z_hi), fsdp: 2 (over z_lo), tensor: 8 (over y, core).
Axes of the slice: x: 4, y: 4, z: 4 (z_hi: 2, z_lo: 2; z = z_hi * 2 + z_lo), core: 2. Of those that a mesh axis runs over, the one named last changes fastest.
Arguments:
- normed: bfloat16 [8192, 8192], P(('gossip', 'fsdp', 'tensor')), may hold values from -24 to 24
- key_cotangent: bfloat16 [8192, 1024], P(('gossip', 'fsdp'), 'tensor'), may hold values from -6 to 6
- value_cotangent: bfloat16 [8192, 1024], P(('gossip', 'fsdp'), 'tensor'), may hold values from -6 to 6
- key_weight: float32 [8, 8192, 1024], P('gossip', 'fsdp', 'tensor'), may hold values from -6 to 6
- value_weight: float32 [8, 8192, 1024], P('gossip', 'fsdp', 'tensor'), may hold values from -6 to 6
- key_momentum: float32 [8, 8192, 1024], P('gossip', 'fsdp', 'tensor'), may hold values from -6 to 6
- value_momentum: float32 [8, 8192, 1024], P('gossip', 'fsdp', 'tensor'), may hold values from -6 to 6
- step_index: int32 [], replicated, may hold values from 0 to 2999
Outputs:
- projected_keys: bfloat16 [8192, 1024], P(('gossip', 'fsdp'), 'tensor')
- projected_values: bfloat16 [8192, 1024], P(('gossip', 'fsdp'), 'tensor')
- input_grad: bfloat16 [8192, 8192], P(('gossip', 'fsdp', 'tensor'))
- new_key_weight: float32 [8, 8192, 1024], P('gossip', 'fsdp', 'tensor')
- new_value_weight: float32 [8, 8192, 1024], P('gossip', 'fsdp', 'tensor')
- new_key_momentum: float32 [8, 8192, 1024], P('gossip', 'fsdp', 'tensor')
- new_value_momentum: float32 [8, 8192, 1024], P('gossip', 'fsdp', 'tensor')
All inputs are finite; a program needn't handle non-finite values.
Results may differ from a plain program's by a relative error of at most 0.0055.
Values may be sent and summed in bfloat16 or wider, within the bound.
No kernel may reach another device: no remote copies, remote signals or barrier semaphores. Data moves between devices by JAX's collectives and lax.ppermute only.
A program may use at most 192 MiB of HBM per device.

v0:
```python
from functools import partial

import jax
import jax.numpy as jnp
from jax import lax
from jax.experimental import pallas as pl
from jax.experimental.pallas import tpu as pltpu
from jax.sharding import PartitionSpec as P

D = 8192
SCALING = D ** (-0.5)
momentum_decay = 0.9
learn_rate = 0.5

F32 = jnp.float32
BF = jnp.bfloat16
HALF = 4096
QUARTER = 2048
CHUNKS = 2
CH = QUARTER // CHUNKS
ROWS = 64
TOK = 512
COLS = 128
TILE = 1024

MB = 1024 * 1024


def sds(shape, dtype):
    return jax.ShapeDtypeStruct(shape, dtype)


def params(mib):
    return pltpu.CompilerParams(vmem_limit_bytes=mib * MB)


def cost(flops, nbytes):
    return pl.CostEstimate(flops=flops // 1000, bytes_accessed=nbytes // 1000, transcendentals=0)


def in_hbm(x):
    return pltpu.with_memory_space_constraint(x, pltpu.HBM)


def by_rows(rows, body, size=128):
    @pl.loop(0, rows // size)
    def _(i):
        body(pl.ds(pl.multiple_of(i * size, size), size))


def smem():
    return pl.BlockSpec(memory_space=pltpu.SMEM)


def vmem():
    return pl.BlockSpec(memory_space=pltpu.VMEM)


def copies(pairs, sems):
    started = [pltpu.make_async_copy(src, dst, sems.at[i]) for i, (src, dst) in enumerate(pairs)]
    for copy in started:
        copy.start()
    for copy in started:
        copy.wait()


def anywhere():
    return pl.BlockSpec(memory_space=pl.ANY)


def split_kernel(where, x, k, v, kv, core_own, core_other, own, other, sems):
    core = (core_own, core_other)
    f, c = where[0], where[2]
    pairs = []
    for g, out in enumerate((own, other)):
        q = 2 * (f + g - 2 * f * g)
        start = pl.multiple_of((q + 1 - c) * QUARTER, QUARTER)
        pairs.append((x.at[:, pl.ds(start, QUARTER)], core[g]))
        start = pl.multiple_of((q + c) * QUARTER, QUARTER)
        pairs.append((x.at[:, pl.ds(start, QUARTER)], out))
    pairs += [(k, kv.at[:, :COLS]), (v, kv.at[:, COLS:])]
    copies(pairs, sems)


def split_inputs(where, x, k, v):
    piece = sds((ROWS, QUARTER), BF)
    return pl.pallas_call(
        split_kernel,
        out_shape=[sds((TOK, 2 * COLS), BF), piece, piece, piece, piece],
        in_specs=[smem()] + [anywhere()] * 3,
        out_specs=[anywhere()] * 5,
        scratch_shapes=[pltpu.SemaphoreType.DMA((6,))],
        compiler_params=params(4),
        cost_estimate=cost(0, 2_600_000),
        name="split_inputs",
    )(where, x, k, v)


def prepare_kernel(where, kw, vw, km, vm, w_own, w_send, *pre):
    h, s = pl.program_id(0), pl.program_id(1)
    halves = ((kw, km, slice(0, COLS)), (vw, vm, slice(COLS, 2 * COLS)))
    for chunk in range(CHUNKS):
        for kind, rounded in ((0, w_own), (1, w_send)):

            @pl.when((h == chunk) & (s == kind))
            def _():
                def body(rows):
                    for w, m, cols in halves:
                        value = w[0, rows, :]
                        pre[chunk][rows, cols] = value - (learn_rate * momentum_decay) * m[0, rows, :]
                        rounded[rows, cols] = value.astype(BF)

                by_rows(TILE, body)


def prepare(where, kw, vw, km, vm):
    n = CH // TILE

    def at(h, s, i, w):
        q = s + w[2] - 2 * s * w[2]
        return (0, (q * CHUNKS + h) * n + i, 0)

    def chunk_at(chunk):
        def index(h, s, i, w):
            inside = s * n + i
            return (jnp.where(h == chunk, inside, jnp.where(h < chunk, 0, 2 * n - 1)), 0)

        return index

    whole = pl.BlockSpec((1, TILE, COLS), at)
    tile = (TILE, 256)
    return pl.pallas_call(
        prepare_kernel,
        out_shape=[sds((QUARTER, 256), BF)] * 2 + [sds((2 * CH, 256), F32)] * CHUNKS,
        grid_spec=pltpu.PrefetchScalarGridSpec(
            num_scalar_prefetch=1,
            grid=(CHUNKS, 2, n),
            in_specs=[whole] * 4,
            out_specs=[
                pl.BlockSpec(tile, lambda h, s, i, w: (h * n + jnp.where(s == 0, i, n - 1), 0)),
                pl.BlockSpec(tile, lambda h, s, i, w: (h * n + jnp.where(s == 1, i, 0), 0)),
            ]
            + [pl.BlockSpec(tile, chunk_at(chunk)) for chunk in range(CHUNKS)],
        ),
        compiler_params=params(24),
        cost_estimate=cost(0, 14 * MB),
        name="prepare_weights",
    )(where, kw, vw, km, vm)


def order_kernel(where, own, core, out):
    y, c = where[1], where[2]
    for j in range(4):
        for cr in range(2):
            t = 2 * lax.rem(y + j, 4) + (c + cr - 2 * c * cr)
            for g in range(2):
                row = pl.multiple_of(t * 2 * ROWS + g * ROWS, ROWS)
                to = j * 256 + g * 128 + cr * ROWS
                out[to : to + ROWS, : 2 * COLS] = own[pl.ds(row, ROWS), :]
                out[to : to + ROWS, 2 * COLS :] = core[pl.ds(row, ROWS), :]


def order_cotangents(where, own, core):
    return pl.pallas_call(
        order_kernel,
        out_shape=sds((1024, 512), BF),
        in_specs=[smem()] + [vmem()] * 2,
        out_specs=vmem(),
        compiler_params=params(8),
        cost_estimate=cost(0, 2 * MB),
        name="order_cotangents",
    )(where, own, core)


NT = (((1,), (1,)), ((), ()))
TN = (((0,), (0,)), ((), ()))
DXT = 1024


def dx_kernel(kv, w0, w1, *outs):
    part = lax.dot_general(kv[:, :256], w0[...], NT, preferred_element_type=F32)
    part += lax.dot_general(kv[:, 256:], w1[...], NT, preferred_element_type=F32)
    part = (part * SCALING).astype(BF)
    for g in range(2):
        for out, chip in zip(outs[4 * g : 4 * g + 4], (2, 1, 3, 0)):
            base = 256 * chip + 128 * (1 - g)
            out[...] = part[base : base + 128]


def input_terms(kv, w0, w1):
    spec = pl.BlockSpec((128, DXT), lambda i: (0, i))
    wspec = pl.BlockSpec((DXT, 256), lambda i: (i, 0))
    return pl.pallas_call(
        dx_kernel,
        out_shape=[sds((128, QUARTER), BF)] * 8,
        grid=(QUARTER // DXT,),
        in_specs=[pl.BlockSpec((1024, 512), lambda i: (0, 0)), wspec, wspec],
        out_specs=[spec] * 8,
        compiler_params=params(24),
        cost_estimate=cost(2 * 1024 * 512 * QUARTER, 7 * MB),
        name="input_terms",
    )(kv, w0, w1)


def dw_kernel(kv, *refs):
    xs, (own, send) = refs[:8], refs[8:]
    x = jnp.concatenate([r[...] for r in xs], axis=0)
    g = lax.dot_general(x, kv[...], TN, preferred_element_type=F32) * SCALING
    own[...] = g[:, :256]
    send[...] = g[:, 256:].astype(BF)


def weight_terms(chunk, kv, xs):
    t = 512
    n = CH // t
    return pl.pallas_call(
        dw_kernel,
        out_shape=[sds((CH, 256), F32), sds((CH, 256), BF)],
        grid=(n,),
        in_specs=[pl.BlockSpec((1024, 512), lambda i: (0, 0))]
        + [pl.BlockSpec((128, t), lambda i: (0, chunk * n + i))] * 8,
        out_specs=[pl.BlockSpec((t, 256), lambda i: (i, 0))] * 2,
        compiler_params=params(24),
        cost_estimate=cost(2 * 1024 * 512 * CH, 5 * MB),
        name="weight_terms",
    )(kv, *xs)


def proj_kernel(*refs):
    xs, (w0, w1), (own, send), acc = refs[:8], refs[8:10], refs[10:12], refs[12]
    i = pl.program_id(0)
    w = jnp.concatenate([w0[...], w1[...]], axis=1)

    @pl.when(i == 0)
    def _():
        acc[...] = jnp.zeros_like(acc)

    for k in range(8):
        rows = slice(128 * k, 128 * k + 128)
        acc[rows] += jnp.dot(xs[k][...], w, preferred_element_type=F32)

    @pl.when(i == pl.num_programs(0) - 1)
    def _():
        own[...] = acc[:, :256] * SCALING
        send[...] = (acc[:, 256:] * SCALING).astype(BF)


def projection(*args):
    t = 512
    wspec = pl.BlockSpec((t, 256), lambda i: (i, 0))
    return pl.pallas_call(
        proj_kernel,
        out_shape=[sds((1024, 256), F32), sds((1024, 256), BF)],
        grid=(QUARTER // t,),
        in_specs=[pl.BlockSpec((128, t), lambda i: (0, i))] * 8 + [wspec] * 2,
        out_specs=[pl.BlockSpec((1024, 256), lambda i: (0, 0))] * 2,
        scratch_shapes=[pltpu.VMEM((1024, 512), F32)],
        compiler_params=params(24),
        cost_estimate=cost(2 * 1024 * 512 * QUARTER, 8 * MB),
        name="projection",
    )(*args)


def proj_sum_kernel(own, got, keep, send):
    for at in range(0, 1024, 64):
        j, o, cr = at // 256, at // 128 % 2, at // 64 % 2
        far = at + 64 - 128 * cr
        total = own[at : at + 64] + got[far : far + 64].astype(F32)
        to = j * 128 + cr * 64
        if o:
            send[to : to + 64] = total.astype(BF)
        else:
            keep[to : to + 64] = total


def projection_sum(own, got):
    return pl.pallas_call(
        proj_sum_kernel,
        out_shape=[sds((512, 256), F32), sds((512, 256), BF)],
        in_specs=[vmem()] * 2,
        out_specs=[vmem()] * 2,
        compiler_params=params(8),
        cost_estimate=cost(0, 2 * MB),
        name="projection_sum",
    )(own, got)


def proj_end_kernel(where, keep, got, keys, values):
    y, c = where[1], where[2]
    for j in range(4):
        for cr in range(2):
            chip = lax.rem(y + j, 4)
            row = pl.multiple_of(chip * 2 * ROWS + (c + cr - 2 * c * cr) * ROWS, ROWS)
            at = j * 128 + cr * ROWS
            total = (keep[at : at + ROWS] + got[at : at + ROWS].astype(F32)).astype(BF)
            keys[pl.ds(row, ROWS), :] = total[:, :COLS]
            values[pl.ds(row, ROWS), :] = total[:, COLS:]


def projection_end(where, keep, got):
    out = pltpu.HBM((512, COLS), BF)
    return pl.pallas_call(
        proj_end_kernel,
        out_shape=[out, out],
        in_specs=[smem()] + [vmem()] * 2,
        out_specs=[vmem()] * 2,
        compiler_params=params(8),
        cost_estimate=cost(0, MB),
        name="projection_end",
    )(where, keep, got)


def sum3_kernel(a, b, c, lo, hi):
    for at, out in ((0, lo), (64, hi)):

        def body(rows):
            far = pl.ds(pl.multiple_of(rows.start + at, 16), rows.size)
            out[rows, :] = (a[far, :].astype(F32) + b[far, :].astype(F32) + c[far, :].astype(F32)).astype(BF)

        by_rows(64, body, 16)


def sum3(a, b, c):
    out = sds((64, QUARTER), BF)
    return pl.pallas_call(
        sum3_kernel,
        out_shape=[out, out],
        in_specs=[vmem()] * 3,
        out_specs=[vmem()] * 2,
        compiler_params=params(8),
        cost_estimate=cost(0, 2 * MB),
        name="sum_terms",
    )(a, b, c)


def join_kernel(where, own, core, z, zc, out):
    f, c = where[0], where[2]
    quarters = (2 * f + c, 2 * f + 1 - c, 2 * (1 - f) + c, 2 * (1 - f) + 1 - c)
    for q, ref in zip(quarters, (own, core, z, zc)):
        out[:, pl.ds(pl.multiple_of(q * QUARTER, QUARTER), QUARTER)] = ref[...]


def join(where, own, core, z, zc):
    return pl.pallas_call(
        join_kernel,
        out_shape=pltpu.HBM((ROWS, D), BF),
        in_specs=[smem()] + [vmem()] * 4,
        out_specs=vmem(),
        compiler_params=params(8),
        cost_estimate=cost(0, 2 * MB),
        name="join_input_grad",
    )(where, own, core, z, zc)


def chunk_specs(chunk):
    n = CH // TILE
    per_quarter = QUARTER // TILE

    def at(s, i, w):
        q = s + w[2] - 2 * s * w[2]
        return (0, q * per_quarter + chunk * n + i, 0)

    whole = pl.BlockSpec((1, TILE, COLS), at)
    term = pl.BlockSpec((TILE, 256), lambda s, i, w: (i, 0))
    moved = pl.BlockSpec((TILE, 256), lambda s, i, w: (s * n + i, 0))
    return (2, n), whole, term, moved


def moved_kernel(pre, own, got, moved):
    def body(rows):
        moved[rows, :] = (pre[rows, :] - learn_rate * own[rows, :]).astype(BF)
        far = pl.ds(pl.multiple_of(rows.start + CH, 128), rows.size)
        moved[far, :] = (pre[far, :] - learn_rate * got[rows, :].astype(F32)).astype(BF)

    by_rows(CH, body)


def moved_chunk(pre, own, got):
    return pl.pallas_call(
        moved_kernel,
        out_shape=sds((2 * CH, 256), BF),
        in_specs=[vmem()] * 3,
        out_specs=vmem(),
        compiler_params=params(8),
        cost_estimate=cost(0, 5 * MB),
        name="moved_weights",
    )(pre, own, got)


def momentum_kernel(where, km, vm, *refs):
    own, got, (nkm, nvm) = refs[:CHUNKS], refs[CHUNKS : 2 * CHUNKS], refs[2 * CHUNKS :]
    s, h = pl.program_id(0), pl.program_id(1)

    def run(g):
        def body(rows):
            nkm[0, rows, :] = momentum_decay * km[0, rows, :] + g[rows, :COLS].astype(F32)
            nvm[0, rows, :] = momentum_decay * vm[0, rows, :] + g[rows, COLS:].astype(F32)

        by_rows(TILE, body)

    for chunk in range(CHUNKS):

        @pl.when((s == 0) & (h == chunk))
        def _():
            run(own[chunk])

        @pl.when((s == 1) & (h == chunk))
        def _():
            run(got[chunk])


def momentum_step(where, km, vm, own, got):
    n = CH // TILE

    def at(s, h, i, w):
        q = s + w[2] - 2 * s * w[2]
        return (0, (q * CHUNKS + h) * n + i, 0)

    whole = pl.BlockSpec((1, TILE, COLS), at)
    terms = [
        pl.BlockSpec(
            (TILE, 256),
            lambda s, h, i, w, kind=kind, chunk=chunk: (jnp.where((s == kind) & (h == chunk), i, 0), 0),
        )
        for kind in range(2)
        for chunk in range(CHUNKS)
    ]
    full = pltpu.HBM((1, HALF, COLS), F32)
    return pl.pallas_call(
        momentum_kernel,
        out_shape=[full, full],
        grid_spec=pltpu.PrefetchScalarGridSpec(
            num_scalar_prefetch=1,
            grid=(2, CHUNKS, n),
            in_specs=[whole] * 2 + terms,
            out_specs=[whole, whole],
        ),
        compiler_params=params(24),
        cost_estimate=cost(0, 11 * MB),
        name="momentum_step",
    )(where, km, vm, *own, *got)


def mean_kernel(where, pre, own, got, partner, *refs):
    nkw, nvw = refs[-2:]
    s = pl.program_id(0)

    def run(g):
        def body(rows):
            mean = 0.5 * ((pre[rows, :] - learn_rate * g[rows, :].astype(F32)) + partner[rows, :].astype(F32))
            nkw[0, rows, :] = mean[:, :COLS]
            nvw[0, rows, :] = mean[:, COLS:]

        by_rows(TILE, body)

    @pl.when(s == 0)
    def _():
        run(own)

    @pl.when(s == 1)
    def _():
        run(got)


def mean(where, chunk, pre, own, got, partner, before):
    grid, whole, term, moved = chunk_specs(chunk)
    full = pltpu.HBM((1, HALF, COLS), F32)
    extra = [] if before is None else list(before)
    return pl.pallas_call(
        mean_kernel,
        out_shape=[full, full],
        grid_spec=pltpu.PrefetchScalarGridSpec(
            num_scalar_prefetch=1,
            grid=grid,
            in_specs=[moved, term, term, moved] + [anywhere()] * len(extra),
            out_specs=[whole, whole],
        ),
        input_output_aliases={5: 0, 6: 1} if extra else {},
        compiler_params=params(24),
        cost_estimate=cost(0, 8 * MB),
        name="average",
    )(where, pre, own, got, partner, *extra)


def to_right(a):
    return lax.ppermute(a, "tensor", [(t, (t + 2) % 8) for t in range(8)])


def to_left(a):
    return lax.ppermute(a, "tensor", [(t, (t + 6) % 8) for t in range(8)])


def to_core(a):
    return lax.ppermute(a, "tensor", [(t, t ^ 1) for t in range(8)])


def to_z(a):
    return lax.ppermute(a, "fsdp", [(0, 1), (1, 0)])


def to_z_core(a):
    return lax.ppermute(a, ("fsdp", "tensor"), [(i, i ^ 9) for i in range(16)])


def to_partner(a, bit):
    n = lax.axis_size("gossip")
    return lax.ppermute(a, "gossip", [(i, i ^ (1 << bit)) for i in range(n)])


def after(value, *others):
    return lax.optimization_barrier((value, others))[0]


def exchange(bit, where, km, vm, kv, pre, terms, xs, w_own, w_core):
    own, send = weight_terms(0, kv, xs)
    got = to_core(send)
    moved = moved_chunk(pre[0], own, got)
    partner = to_partner(moved, bit)
    o_terms, s_terms = terms[:4], terms[4:]
    o_left = to_left(o_terms[2])
    o_relayed = o_terms[1] + to_right(o_terms[0])
    own1, send = weight_terms(1, after(kv, own), xs)
    got1 = to_core(send)
    p_own, p_send = projection(*xs, w_own, w_core)
    o_right = to_right(after(o_relayed, p_send))
    keep, p_send = projection_sum(p_own, to_core(p_send))
    p_z = to_z(p_send)
    partner1 = to_partner(after(moved_chunk(pre[1], own1, got1), keep), bit)
    keys, values = projection_end(where, keep, p_z)
    o_z, o_zc = sum3(o_terms[3], o_right, o_left)
    z, zc = to_z(o_z), to_z_core(o_zc)
    weights = mean(where, 0, pre[0], own, got, partner, None)
    s_left = to_left(after(s_terms[2] + to_left(after(s_terms[0], o_left)), o_z, weights[0]))
    s_right = to_right(after(s_terms[1], o_right, p_z if bit else p_send))
    momenta = momentum_step(after(where, o_z), km, vm, (own, own1), (got, got1))
    s_own, s_core = sum3(after(s_terms[3], momenta, weights), s_right, s_left)
    parts = (s_own, to_core(s_core), z, zc)
    if bit:
        input_grad = join(where, *parts)
        partner1 = after(partner1, input_grad)
    weights = mean(where, 1, pre[1], own1, got1, partner1, weights)
    if not bit:
        input_grad = join(where, *after(parts, weights[0]))
    return keys, values, input_grad, *weights, *momenta


def per_device(normed, kc, vc, kw, vw, km, vm, step_index):
    t = lax.axis_index("tensor")
    where = jnp.stack([lax.axis_index("fsdp"), t // 2, t % 2]).astype(jnp.int32)
    levels = lax.axis_size("gossip").bit_length() - 1
    bit = step_index % levels

    normed, kc, vc, kw, vw, km, vm = map(in_hbm, (normed, kc, vc, kw, vw, km, vm))
    kv_own, x_core, z_core, x_own, x_z = split_inputs(where, normed, kc, vc)
    x_core = to_core(x_core)
    a = jnp.concatenate([x_own, x_core], axis=0)
    b = jnp.concatenate([to_z(x_z), to_z_core(z_core)], axis=0)
    a3, a1 = to_right(a), to_left(a)
    w_own, w_send, *pre = prepare(after(where, a), kw, vw, km, vm)
    a3, b, w_own, w_send = lax.optimization_barrier((a3, b, w_own, w_send))
    a1, kv_own = lax.optimization_barrier((a1, kv_own))
    a2 = to_right(a3)
    kv_z = to_z(kv_own)
    b3, b1 = to_right(b), to_left(b)
    b2 = to_left(b1)
    kv = jnp.stack([kv_own.reshape(8, ROWS, 256), kv_z.reshape(8, ROWS, 256)], axis=1).reshape(1024, 256)
    kv = after(kv, a2)
    kv = order_cotangents(where, kv, to_core(kv))
    w_core = to_core(w_send)
    terms = input_terms(kv, w_own, w_core)
    xs = (a, b, a1, b1, a2, b2, a3, b3)
    kv = after(kv, terms[0])
    return lax.switch(
        bit,
        [partial(exchange, k) for k in range(levels)],
        where, km, vm, kv, pre, terms, xs, w_own, w_core,
    )


def solution(mesh):
    rows = P(("gossip", "fsdp", "tensor"), None)
    heads = P(("gossip", "fsdp"), "tensor")
    weight = P("gossip", "fsdp", "tensor")
    return jax.shard_map(
        per_device,
        mesh=mesh,
        in_specs=(rows, heads, heads, weight, weight, weight, weight, P()),
        out_specs=(heads, heads, rows, weight, weight, weight, weight),
        check_vma=False,
    )
```

profile of v0, /device:TPU:1, one launch (start us, length us, event | category | flops | bytes accessed | tf_op | source)
XLA Modules:
  0.0 108.0 jit_solution(10467748354643514902)
XLA Ops:
  0.7 1.9 %split_inputs.1 = (bf16[512,256]{1,0:T(8,128)(2,1)S(1)}, bf16[64,2048]{1,0:T(8,128)(2,1)S(1)}, bf16[64,2048]{1,0:T(8,128)(2,1)S(1)}, bf16[64,2048]{1,0:T(8,128)(2,1)S(1)}, bf16[64,2048]{1,0:T(8,128)(2,1)S(1)}) custom-call(s32[3]{0:T(128)S(1)} %pad_add_fusion.where, bf16[64,8192]{1,0:T(8,128)(2,1)} %x.1, bf16[512,128]{1,0:T(8,128)(2,1)} %k.1, bf16[512,128]{1,0:T(8,128)(2,1)} %v.1), custom_call_target="tpu_custom_call" | custom-call | bytes 2600 | tf_op jit(solution)/shard_map/split_inputs/pallas_call | solution.py:87
  6.7 1.6 %collective-permute-start.47 = (bf16[64,2048]{1,0:T(8,128)(2,1)S(1)}, bf16[64,2048]{1,0:T(8,128)(2,1)S(1)}, u32[]{:S(2)}, u32[]{:S(2)}) collective-permute-start(bf16[64,2048]{1,0:T(8,128)(2,1)S(1)} %get-tuple-element.341), channel_id=1, source_target_pairs={{0,8},{8,0},{1,9},{9,1},{2,10},{10,2},{3,11},{11,3},{4,12},{12,4},... | collective-permute-start | bytes 786440 | tf_op jit(solution)/shard_map/ppermute | solution.py:498
  10.3 6.8 %prepare_weights.1 = (bf16[2048,256]{1,0:T(8,128)(2,1)}, bf16[2048,256]{1,0:T(8,128)(2,1)S(1)}, f32[2048,256]{1,0:T(8,128)}, f32[2048,256]{1,0:T(8,128)}) custom-call(s32[3]{0:T(128)S(1)} %pad_add_fusion.where, f32[1,4096,128]{2,1,0:T(8,128)} %kw.1, f32[1,4096,128]{2,1,0:T(8,128)} %vw.1, f32[1,4096,128]{2,1,0:T(8,128)} %km.1, f32[1,4096,128]{2,1,0:T(8,128)} %vm.1), custom_call_target="tpu_custom_call" | custom-call | bytes 14680 | tf_op jit(solution)/shard_map/prepare_weights/pallas_call | solution.py:132
  17.2 3.7 %collective-permute-done.48 = bf16[64,2048]{1,0:T(8,128)(2,1)S(1)} collective-permute-done((bf16[64,2048]{1,0:T(8,128)(2,1)S(1)}, bf16[64,2048]{1,0:T(8,128)(2,1)S(1)}, u32[]{:S(2)}, u32[]{:S(2)}) %collective-permute-start.48) | collective-permute-done | bytes 262176 | tf_op jit(solution)/shard_map/ppermute | solution.py:502
  25.9 5.7 %collective-permute-done.55 = bf16[512,256]{1,0:T(8,128)(2,1)S(1)} collective-permute-done((bf16[512,256]{1,0:T(8,128)(2,1)S(1)}, bf16[512,256]{1,0:T(8,128)(2,1)S(1)}, u32[]{:S(2)}, u32[]{:S(2)}) %collective-permute-start.55) | collective-permute-done | bytes 262176 | tf_op jit(solution)/shard_map/ppermute | solution.py:498
  31.6 5.2 %collective-permute-done.51 = bf16[128,2048]{1,0:T(8,128)(2,1)} collective-permute-done((bf16[128,2048]{1,0:T(8,128)(2,1)S(1)}, bf16[128,2048]{1,0:T(8,128)(2,1)}, u32[]{:S(2)}, u32[]{:S(2)}) %collective-permute-start.51) | collective-permute-done | bytes 524320 | tf_op jit(solution)/shard_map/ppermute | solution.py:486
  37.5 2.6 %collective-permute-start.52 = (bf16[128,2048]{1,0:T(8,128)(2,1)}, bf16[128,2048]{1,0:T(8,128)(2,1)}, u32[]{:S(2)}, u32[]{:S(2)}) collective-permute-start(bf16[128,2048]{1,0:T(8,128)(2,1)} %collective-permute-done.50), channel_id=1, source_target_pairs={{0,6},{1,7},{2,0},{3,1},{4,2},{5,3},{6,4},{7,5},{8,14},{9,15},{10,... | collective-permute-start | bytes 1572872 | tf_op jit(solution)/shard_map/ppermute | solution.py:490
  41.4 4.3 %input_terms.1 = (bf16[128,2048]{1,0:T(8,128)(2,1)S(1)}, bf16[128,2048]{1,0:T(8,128)(2,1)S(1)}, bf16[128,2048]{1,0:T(8,128)(2,1)S(1)}, bf16[128,2048]{1,0:T(8,12...) custom-call(bf16[1024,512]{1,0:T(8,128)(2,1)S(1)} %order_cotangents., ...), custom_call_target="tpu_custom_call" | custom-call | flops 2147483 | bytes 7340 | tf_op jit(solution)/shard_map/input_terms/pallas_call | solution.py:193
  45.7 6.7 %collective-permute-done.53 = bf16[128,2048]{1,0:T(8,128)(2,1)} collective-permute-done((bf16[128,2048]{1,0:T(8,128)(2,1)}, bf16[128,2048]{1,0:T(8,128)(2,1)}, u32[]{:S(2)}, u32[]{:S(2)}) %collective-permute-start.53) | collective-permute-done | bytes 524320 | tf_op jit(solution)/shard_map/ppermute | solution.py:486
  52.4 55.7 %conditional.1 = (bf16[512,128]{1,0:T(8,128)(2,1)}, bf16[512,128]{1,0:T(8,128)(2,1)}, f32[1,4096,128]{2,1,0:T(8,128)}, f32[1,4096,128]{2,1,0:T(8,128)}, f32[1,40...) conditional(s32[]{:T(128)} %clamp.3, ...), branch_computations={%region_0.1_spmd, %region_1.2_spmd, %region_2.3_spmd} | conditional | flops 4819253 | bytes 40962276 | solution.py:573
  52.6 2.8 %weight_terms.8 = (f32[1024,256]{1,0:T(8,128)S(1)}, bf16[1024,256]{1,0:T(8,128)(2,1)S(1)}) custom-call(bf16[1024,512]{1,0:T(8,128)(2,1)S(1)} %get-tuple-element.229.kv, bf16[128,2048]{1,0:T(8,128)(2,1)S(1)} %get-tuple-element.201.refs_0_, bf16[128,2048]{1,0:T(8,128)(2,1)} %get-tuple-element.202.refs_1_, bf16[128,2048]{1,0:T(8,128)(2,1)} %get-tuple-element.203.refs_2_, ...), custom_call_target="tpu_custom_call" | custom-call | flops 1073741 | bytes 5242 | tf_op jit(solution)/shard_map/cond/branch_1_fun/weight_terms/pallas_call | solution.py:216
  56.3 2.7 %collective-permute-start.19 = (bf16[128,2048]{1,0:T(8,128)(2,1)S(1)}, bf16[128,2048]{1,0:T(8,128)(2,1)S(1)}, u32[]{:S(2)}, u32[]{:S(2)}) collective-permute-start(bf16[128,2048]{1,0:T(8,128)(2,1)S(1)} %get-tuple-element.222), channel_id=1, source_target_pairs={{0,6},{1,7},{2,0},{3,1},{4,2},{5,3},{6,4},{7,5},{8,14},{9,15},{10,... | collective-permute-start | bytes 1572872 | tf_op jit(solution)/shard_map/cond/branch_1_fun/ppermute | solution.py:490
  60.6 5.2 %projection.4 = (f32[1024,256]{1,0:T(8,128)S(1)}, bf16[1024,256]{1,0:T(8,128)(2,1)S(1)}) custom-call(bf16[128,2048]{1,0:T(8,128)(2,1)S(1)} %get-tuple-element.201.refs_0_, bf16[128,2048]{1,0:T(8,128)(2,1)} %get-tuple-element.202.refs_1_, bf16[128,2048]{1,0:T(8,128)(2,1)S(1)} %copy-done.8, bf16[128,2048]{1,0:T(8,128)(2,1)} %get-tuple-element.204.refs_3_, ...), custom_call_target="tpu_custom_call" | custom-call | flops 2147483 | bytes 8388 | tf_op jit(solution)/shard_map/cond/branch_1_fun/projection/pallas_call | solution.py:251
  66.8 2.7 %weight_terms.9 = (f32[1024,256]{1,0:T(8,128)S(1)}, bf16[1024,256]{1,0:T(8,128)(2,1)S(1)}) custom-call(bf16[1024,512]{1,0:T(8,128)(2,1)S(1)} %get-tuple-element.229.kv, bf16[128,2048]{1,0:T(8,128)(2,1)S(1)} %get-tuple-element.201.refs_0_, bf16[128,2048]{1,0:T(8,128)(2,1)} %get-tuple-element.202.refs_1_, bf16[128,2048]{1,0:T(8,128)(2,1)S(1)} %copy-done.8, ...), custom_call_target="tpu_custom_call" | custom-call | flops 1073741 | bytes 5242 | tf_op jit(solution)/shard_map/cond/branch_1_fun/weight_terms/pallas_call | solution.py:216
  71.2 2.7 %collective-permute-start.24 = (bf16[128,2048]{1,0:T(8,128)(2,1)S(1)}, bf16[128,2048]{1,0:T(8,128)(2,1)S(1)}, u32[]{:S(2)}, u32[]{:S(2)}) collective-permute-start(bf16[128,2048]{1,0:T(8,128)(2,1)S(1)} %get-tuple-element.243), channel_id=1, source_target_pairs={{0,6},{1,7},{2,0},{3,1},{4,2},{5,3},{6,4},{7,5},{8,14},{9,15},{10,... | collective-permute-start | bytes 1572872 | tf_op jit(solution)/shard_map/cond/branch_1_fun/ppermute | solution.py:490
  77.1 3.4 %collective-permute-done.16.got = bf16[512,256]{1,0:T(8,128)(2,1)S(1)} collective-permute-done((bf16[512,256]{1,0:T(8,128)(2,1)S(1)}, bf16[512,256]{1,0:T(8,128)(2,1)S(1)}, u32[]{:S(2)}, u32[]{:S(2)}) %collective-permute-start.16) | collective-permute-done | bytes 262176 | tf_op jit(solution)/shard_map/cond/branch_1_fun/ppermute | solution.py:498
  80.5 4.6 %collective-permute-done.18.b = bf16[128,2048]{1,0:T(8,128)(2,1)S(1)} collective-permute-done((bf16[128,2048]{1,0:T(8,128)(2,1)S(1)}, bf16[128,2048]{1,0:T(8,128)(2,1)S(1)}, u32[]{:S(2)}, u32[]{:S(2)}) %collective-permute-start.18) | collective-permute-done | bytes 524320 | tf_op jit(solution)/shard_map/cond/branch_1_fun/ppermute | solution.py:486
  85.4 2.1 %average.8 = (f32[1,4096,128]{2,1,0:T(8,128)}, f32[1,4096,128]{2,1,0:T(8,128)}) custom-call(s32[3]{0:T(128)S(1)} %get-tuple-element.224.where, f32[2048,256]{1,0:T(8,128)S(1)} %get-tuple-element.235.pre, f32[1024,256]{1,0:T(8,128)S(1)} %get-tuple-element.228.refs_0_.own, bf16[1024,256]{1,0:T(8,128)(2,1)S(1)} %collective-permute-done.20.refs_2_.got, ...), custom_call_target="tpu_custom_call" | custom-call | bytes 8388 | tf_op jit(solution)/shard_map/cond/branch_1_fun/average/pallas_call | solution.py:469
  87.5 2.7 %collective-permute-start.25 = (bf16[128,2048]{1,0:T(8,128)(2,1)S(1)}, bf16[128,2048]{1,0:T(8,128)(2,1)S(1)}, u32[]{:S(2)}, u32[]{:S(2)}) collective-permute-start(bf16[128,2048]{1,0:T(8,128)(2,1)S(1)} %add.21), channel_id=1, source_target_pairs={{0,6},{1,7},{2,0},{3,1},{4,2},{5,3},{6,4},{7,5},{8,14},{9,15},{10,... | collective-permute-start | bytes 1572872 | tf_op jit(solution)/shard_map/cond/branch_1_fun/ppermute | solution.py:490
  91.7 2.5 %collective-permute-start.28 = (bf16[64,2048]{1,0:T(8,128)(2,1)S(1)}, bf16[64,2048]{1,0:T(8,128)(2,1)S(1)}, u32[]{:S(2)}, u32[]{:S(2)}) collective-permute-start(bf16[64,2048]{1,0:T(8,128)(2,1)S(1)} %get-tuple-element.247), channel_id=1, source_target_pairs={{0,9},{1,8},{2,11},{3,10},{4,13},{5,12},{6,15},{7,14},{8,1},{9,0},... | collective-permute-start | bytes 786440 | tf_op jit(solution)/shard_map/cond/branch_1_fun/ppermute | solution.py:502
  94.2 5.4 %momentum_step.4 = (f32[1,4096,128]{2,1,0:T(8,128)}, f32[1,4096,128]{2,1,0:T(8,128)}) custom-call(s32[3]{0:T(128)S(1)} %get-tuple-element.224.where, f32[1,4096,128]{2,1,0:T(8,128)} %get-tuple-element.225.km, f32[1,4096,128]{2,1,0:T(8,128)} %get-tuple-element.226.vm, f32[1024,256]{1,0:T(8,128)S(1)} %get-tuple-element.228.refs_0_.own, ...), custom_call_target="tpu_custom_call" | custom-call | bytes 11534 | tf_op jit(solution)/shard_map/cond/branch_1_fun/momentum_step/pallas_call | solution.py:429
  99.8 2.8 %collective-permute-start.26 = (bf16[64,2048]{1,0:T(8,128)(2,1)S(1)}, bf16[64,2048]{1,0:T(8,128)(2,1)S(1)}, u32[]{:S(2)}, u32[]{:S(2)}) collective-permute-start(bf16[64,2048]{1,0:T(8,128)(2,1)S(1)} %get-tuple-element.246), channel_id=1, source_target_pairs={{0,1},{1,0},{2,3},{3,2},{4,5},{5,4},{6,7},{7,6},{8,9},{9,8},{10,11... | collective-permute-start | bytes 786440 | tf_op jit(solution)/shard_map/cond/branch_1_fun/ppermute | solution.py:494
  104.2 1.6 %join_input_grad.4 = bf16[64,8192]{1,0:T(8,128)(2,1)} custom-call(s32[3]{0:T(128)S(1)} %get-tuple-element.224.where, bf16[64,2048]{1,0:T(8,128)(2,1)S(1)} %get-tuple-element.245.own, bf16[64,2048]{1,0:T(8,128)(2,1)S(1)} %collective-permute-done.26.core, bf16[64,2048]{1,0:T(8,128)(2,1)S(1)} %collective-permute-done.27.z, ...), custom_call_target="tpu_custom_call" | custom-call | bytes 2097 | tf_op jit(solution)/shard_map/cond/branch_1_fun/join_input_grad/pallas_call | solution.py:344
  105.9 2.1 %average.9 = (f32[1,4096,128]{2,1,0:T(8,128)}, f32[1,4096,128]{2,1,0:T(8,128)}) custom-call(s32[3]{0:T(128)S(1)} %get-tuple-element.224.where, f32[2048,256]{1,0:T(8,128)S(1)} %get-tuple-element.248.pre, f32[1024,256]{1,0:T(8,128)S(1)} %get-tuple-element.230.refs_1_.own, ...), custom_call_target="tpu_custom_call", output_to_operand_aliasing={{0}: (5, {}), {1}: (6, {})} | custom-call | bytes 8388 | tf_op jit(solution)/shard_map/cond/branch_1_fun/average/pallas_call | solution.py:469
  (73 shorter events, 24.6 us)
Async XLA Ops:
  5.3 16.4 %collective-permute-start.46 = (bf16[128,2048]{1,0:T(8,128)(2,1)S(1)}, bf16[128,2048]{1,0:T(8,128)(2,1)S(1)}, u32[]{:S(2)}, u32[]{:S(2)}) collective-permute-start(bf16[128,2048]{1,0:T(8,128)(2,1)S(1)} %constant_dynamic-update-slice_fusion), channel_id=1, source_target_pairs={{0,2},{1,3},{2,4},{3,5},{4,6},{5,7},{6,0},{7,1},{8,10},{9,11},{10,... | collective-permute-start | bytes 1572872 | tf_op jit(solution)/shard_map/ppermute | solution.py:486
  6.7 10.4 %collective-permute-start.47 = (bf16[64,2048]{1,0:T(8,128)(2,1)S(1)}, bf16[64,2048]{1,0:T(8,128)(2,1)S(1)}, u32[]{:S(2)}, u32[]{:S(2)}) collective-permute-start(bf16[64,2048]{1,0:T(8,128)(2,1)S(1)} %get-tuple-element.341), channel_id=1, source_target_pairs={{0,8},{8,0},{1,9},{9,1},{2,10},{10,2},{3,11},{11,3},{4,12},{12,4},... | collective-permute-start | bytes 786440 | tf_op jit(solution)/shard_map/ppermute | solution.py:498
  8.4 12.5 %collective-permute-start.48 = (bf16[64,2048]{1,0:T(8,128)(2,1)S(1)}, bf16[64,2048]{1,0:T(8,128)(2,1)S(1)}, u32[]{:S(2)}, u32[]{:S(2)}) collective-permute-start(bf16[64,2048]{1,0:T(8,128)(2,1)S(1)} %get-tuple-element.342), channel_id=1, source_target_pairs={{0,9},{1,8},{2,11},{3,10},{4,13},{5,12},{6,15},{7,14},{8,1},{9,0},... | collective-permute-start | bytes 786440 | tf_op jit(solution)/shard_map/ppermute | solution.py:502
  9.0 15.4 %collective-permute-start.49 = (bf16[128,2048]{1,0:T(8,128)(2,1)S(1)}, bf16[128,2048]{1,0:T(8,128)(2,1)S(1)}, u32[]{:S(2)}, u32[]{:S(2)}) collective-permute-start(bf16[128,2048]{1,0:T(8,128)(2,1)S(1)} %constant_dynamic-update-slice_fusion), channel_id=1, source_target_pairs={{0,6},{1,7},{2,0},{3,1},{4,2},{5,3},{6,4},{7,5},{8,14},{9,15},{10,... | collective-permute-start | bytes 1572872 | tf_op jit(solution)/shard_map/ppermute | solution.py:490
  21.7 15.1 %collective-permute-start.51 = (bf16[128,2048]{1,0:T(8,128)(2,1)S(1)}, bf16[128,2048]{1,0:T(8,128)(2,1)}, u32[]{:S(2)}, u32[]{:S(2)}) collective-permute-start(bf16[128,2048]{1,0:T(8,128)(2,1)S(1)} %collective-permute-done.46), channel_id=1, source_target_pairs={{0,2},{1,3},{2,4},{3,5},{4,6},{5,7},{6,0},{7,1},{8,10},{9,11},{10,... | collective-permute-start | bytes 1572872 | tf_op jit(solution)/shard_map/ppermute | solution.py:486
  23.0 18.4 %collective-permute-start.54 = (bf16[2048,256]{1,0:T(8,128)(2,1)S(1)}, bf16[2048,256]{1,0:T(8,128)(2,1)}, u32[]{:S(2)}, u32[]{:S(2)}) collective-permute-start(bf16[2048,256]{1,0:T(8,128)(2,1)S(1)} %get-tuple-element.351), channel_id=1, source_target_pairs={{0,1},{1,0},{2,3},{3,2},{4,5},{5,4},{6,7},{7,6},{8,9},{9,8},{10,11... | collective-permute-start | bytes 3145736 | tf_op jit(solution)/shard_map/ppermute | solution.py:494
  23.0 14.5 %collective-permute-start.50 = (bf16[128,2048]{1,0:T(8,128)(2,1)}, bf16[128,2048]{1,0:T(8,128)(2,1)}, u32[]{:S(2)}, u32[]{:S(2)}) collective-permute-start(bf16[128,2048]{1,0:T(8,128)(2,1)} %pad_maximum_fusion), channel_id=1, source_target_pairs={{0,6},{1,7},{2,0},{3,1},{4,2},{5,3},{6,4},{7,5},{8,14},{9,15},{10,... | collective-permute-start | bytes 1572872 | tf_op jit(solution)/shard_map/ppermute | solution.py:490
  24.4 7.1 %collective-permute-start.55 = (bf16[512,256]{1,0:T(8,128)(2,1)S(1)}, bf16[512,256]{1,0:T(8,128)(2,1)S(1)}, u32[]{:S(2)}, u32[]{:S(2)}) collective-permute-start(bf16[512,256]{1,0:T(8,128)(2,1)S(1)} %get-tuple-element.352), channel_id=1, source_target_pairs={{0,8},{8,0},{1,9},{9,1},{2,10},{10,2},{3,11},{11,3},{4,12},{12,4},... | collective-permute-start | bytes 786440 | tf_op jit(solution)/shard_map/ppermute | solution.py:498
  37.4 15.0 %collective-permute-start.53 = (bf16[128,2048]{1,0:T(8,128)(2,1)}, bf16[128,2048]{1,0:T(8,128)(2,1)}, u32[]{:S(2)}, u32[]{:S(2)}) collective-permute-start(bf16[128,2048]{1,0:T(8,128)(2,1)} %pad_maximum_fusion), channel_id=1, source_target_pairs={{0,2},{1,3},{2,4},{3,5},{4,6},{5,7},{6,0},{7,1},{8,10},{9,11},{10,... | collective-permute-start | bytes 1572872 | tf_op jit(solution)/shard_map/ppermute | solution.py:486
  37.5 14.9 %collective-permute-start.52 = (bf16[128,2048]{1,0:T(8,128)(2,1)}, bf16[128,2048]{1,0:T(8,128)(2,1)}, u32[]{:S(2)}, u32[]{:S(2)}) collective-permute-start(bf16[128,2048]{1,0:T(8,128)(2,1)} %collective-permute-done.50), channel_id=1, source_target_pairs={{0,6},{1,7},{2,0},{3,1},{4,2},{5,3},{6,4},{7,5},{8,14},{9,15},{10,... | collective-permute-start | bytes 1572872 | tf_op jit(solution)/shard_map/ppermute | solution.py:490
  56.3 14.7 %collective-permute-start.17 = (bf16[128,2048]{1,0:T(8,128)(2,1)S(1)}, bf16[128,2048]{1,0:T(8,128)(2,1)S(1)}, u32[]{:S(2)}, u32[]{:S(2)}) collective-permute-start(bf16[128,2048]{1,0:T(8,128)(2,1)S(1)} %get-tuple-element.220), channel_id=1, source_target_pairs={{0,2},{1,3},{2,4},{3,5},{4,6},{5,7},{6,0},{7,1},{8,10},{9,11},{10,... | collective-permute-start | bytes 1572872 | tf_op jit(solution)/shard_map/cond/branch_1_fun/ppermute | solution.py:486
  56.3 14.9 %collective-permute-start.19 = (bf16[128,2048]{1,0:T(8,128)(2,1)S(1)}, bf16[128,2048]{1,0:T(8,128)(2,1)S(1)}, u32[]{:S(2)}, u32[]{:S(2)}) collective-permute-start(bf16[128,2048]{1,0:T(8,128)(2,1)S(1)} %get-tuple-element.222), channel_id=1, source_target_pairs={{0,6},{1,7},{2,0},{3,1},{4,2},{5,3},{6,4},{7,5},{8,14},{9,15},{10,... | collective-permute-start | bytes 1572872 | tf_op jit(solution)/shard_map/cond/branch_1_fun/ppermute | solution.py:490
  59.3 26.1 %collective-permute-start.22 = (bf16[2048,256]{1,0:T(8,128)(2,1)S(1)}, bf16[2048,256]{1,0:T(8,128)(2,1)S(1)}, u32[]{:S(2)}, u32[]{:S(2)}) collective-permute-start(bf16[2048,256]{1,0:T(8,128)(2,1)S(1)} %moved_weights.8), channel_id=1, source_target_pairs={{0,32},{16,48},{32,0},{48,16},{64,96},{80,112},{96,64},{112,80},{1... | collective-permute-start | bytes 3145736 | tf_op jit(solution)/shard_map/cond/branch_1_fun/ppermute | solution.py:507
  65.8 8.1 %collective-permute-start.15 = (bf16[1024,256]{1,0:T(8,128)(2,1)S(1)}, bf16[1024,256]{1,0:T(8,128)(2,1)S(1)}, u32[]{:S(2)}, u32[]{:S(2)}) collective-permute-start(bf16[1024,256]{1,0:T(8,128)(2,1)S(1)} %get-tuple-element.212), channel_id=1, source_target_pairs={{0,1},{1,0},{2,3},{3,2},{4,5},{5,4},{6,7},{7,6},{8,9},{9,8},{10,11... | collective-permute-start | bytes 1572872 | tf_op jit(solution)/shard_map/cond/branch_1_fun/ppermute | solution.py:494
  69.5 6.0 %collective-permute-start.21 = (bf16[1024,256]{1,0:T(8,128)(2,1)S(1)}, bf16[1024,256]{1,0:T(8,128)(2,1)S(1)}, u32[]{:S(2)}, u32[]{:S(2)}) collective-permute-start(bf16[1024,256]{1,0:T(8,128)(2,1)S(1)} %get-tuple-element.232), channel_id=1, source_target_pairs={{0,1},{1,0},{2,3},{3,2},{4,5},{5,4},{6,7},{7,6},{8,9},{9,8},{10,11... | collective-permute-start | bytes 1572872 | tf_op jit(solution)/shard_map/cond/branch_1_fun/ppermute | solution.py:494
  71.2 13.9 %collective-permute-start.18 = (bf16[128,2048]{1,0:T(8,128)(2,1)S(1)}, bf16[128,2048]{1,0:T(8,128)(2,1)S(1)}, u32[]{:S(2)}, u32[]{:S(2)}) collective-permute-start(bf16[128,2048]{1,0:T(8,128)(2,1)S(1)} %add.20), channel_id=1, source_target_pairs={{0,2},{1,3},{2,4},{3,5},{4,6},{5,7},{6,0},{7,1},{8,10},{9,11},{10,... | collective-permute-start | bytes 1572872 | tf_op jit(solution)/shard_map/cond/branch_1_fun/ppermute | solution.py:486
  71.2 14.0 %collective-permute-start.24 = (bf16[128,2048]{1,0:T(8,128)(2,1)S(1)}, bf16[128,2048]{1,0:T(8,128)(2,1)S(1)}, u32[]{:S(2)}, u32[]{:S(2)}) collective-permute-start(bf16[128,2048]{1,0:T(8,128)(2,1)S(1)} %get-tuple-element.243), channel_id=1, source_target_pairs={{0,6},{1,7},{2,0},{3,1},{4,2},{5,3},{6,4},{7,5},{8,14},{9,15},{10,... | collective-permute-start | bytes 1572872 | tf_op jit(solution)/shard_map/cond/branch_1_fun/ppermute | solution.py:490
  74.0 6.5 %collective-permute-start.16 = (bf16[512,256]{1,0:T(8,128)(2,1)S(1)}, bf16[512,256]{1,0:T(8,128)(2,1)S(1)}, u32[]{:S(2)}, u32[]{:S(2)}) collective-permute-start(bf16[512,256]{1,0:T(8,128)(2,1)S(1)} %get-tuple-element.214), channel_id=1, source_target_pairs={{0,8},{8,0},{1,9},{9,1},{2,10},{10,2},{3,11},{11,3},{4,12},{12,4},... | collective-permute-start | bytes 786440 | tf_op jit(solution)/shard_map/cond/branch_1_fun/ppermute | solution.py:498
  75.8 30.1 %collective-permute-start.29 = (bf16[2048,256]{1,0:T(8,128)(2,1)S(1)}, bf16[2048,256]{1,0:T(8,128)(2,1)S(1)}, u32[]{:S(2)}, u32[]{:S(2)}) collective-permute-start(bf16[2048,256]{1,0:T(8,128)(2,1)S(1)} %moved_weights.9), channel_id=1, source_target_pairs={{0,32},{16,48},{32,0},{48,16},{64,96},{80,112},{96,64},{112,80},{1... | collective-permute-start | bytes 3145736 | tf_op jit(solution)/shard_map/cond/branch_1_fun/ppermute | solution.py:507
  85.0 14.6 %collective-permute-start.23 = (bf16[128,2048]{1,0:T(8,128)(2,1)S(1)}, bf16[128,2048]{1,0:T(8,128)(2,1)S(1)}, u32[]{:S(2)}, u32[]{:S(2)}) collective-permute-start(bf16[128,2048]{1,0:T(8,128)(2,1)S(1)} %get-tuple-element.240), channel_id=1, source_target_pairs={{0,2},{1,3},{2,4},{3,5},{4,6},{5,7},{6,0},{7,1},{8,10},{9,11},{10,... | collective-permute-start | bytes 1572872 | tf_op jit(solution)/shard_map/cond/branch_1_fun/ppermute | solution.py:486
  87.5 12.1 %collective-permute-start.25 = (bf16[128,2048]{1,0:T(8,128)(2,1)S(1)}, bf16[128,2048]{1,0:T(8,128)(2,1)S(1)}, u32[]{:S(2)}, u32[]{:S(2)}) collective-permute-start(bf16[128,2048]{1,0:T(8,128)(2,1)S(1)} %add.21), channel_id=1, source_target_pairs={{0,6},{1,7},{2,0},{3,1},{4,2},{5,3},{6,4},{7,5},{8,14},{9,15},{10,... | collective-permute-start | bytes 1572872 | tf_op jit(solution)/shard_map/cond/branch_1_fun/ppermute | solution.py:490
  90.2 13.9 %collective-permute-start.27 = (bf16[64,2048]{1,0:T(8,128)(2,1)S(1)}, bf16[64,2048]{1,0:T(8,128)(2,1)S(1)}, u32[]{:S(2)}, u32[]{:S(2)}) collective-permute-start(bf16[64,2048]{1,0:T(8,128)(2,1)S(1)} %get-tuple-element.223), channel_id=1, source_target_pairs={{0,8},{8,0},{1,9},{9,1},{2,10},{10,2},{3,11},{11,3},{4,12},{12,4},... | collective-permute-start | bytes 786440 | tf_op jit(solution)/shard_map/cond/branch_1_fun/ppermute | solution.py:498
  91.7 12.5 %collective-permute-start.28 = (bf16[64,2048]{1,0:T(8,128)(2,1)S(1)}, bf16[64,2048]{1,0:T(8,128)(2,1)S(1)}, u32[]{:S(2)}, u32[]{:S(2)}) collective-permute-start(bf16[64,2048]{1,0:T(8,128)(2,1)S(1)} %get-tuple-element.247), channel_id=1, source_target_pairs={{0,9},{1,8},{2,11},{3,10},{4,13},{5,12},{6,15},{7,14},{8,1},{9,0},... | collective-permute-start | bytes 786440 | tf_op jit(solution)/shard_map/cond/branch_1_fun/ppermute | solution.py:502
  99.8 4.3 %collective-permute-start.26 = (bf16[64,2048]{1,0:T(8,128)(2,1)S(1)}, bf16[64,2048]{1,0:T(8,128)(2,1)S(1)}, u32[]{:S(2)}, u32[]{:S(2)}) collective-permute-start(bf16[64,2048]{1,0:T(8,128)(2,1)S(1)} %get-tuple-element.246), channel_id=1, source_target_pairs={{0,1},{1,0},{2,3},{3,2},{4,5},{5,4},{6,7},{7,6},{8,9},{9,8},{10,11... | collective-permute-start | bytes 786440 | tf_op jit(solution)/shard_map/cond/branch_1_fun/ppermute | solution.py:494
  (12 other events, 97.4 us)
where the time goes:
time: 109 us; the launch traced here: 108 us
  Pallas kernels  37.8 us (35%)
  starting transfers between devices  34.9 us (32%)
  waiting for transfers between devices  32.2 us (30%)
  between operations  1.45 us (1%)
  other arithmetic  1.21 us (1%)
    ppermute x6, waiting for transfers between devices, to_right(): return lax.ppermute(a, 'tensor', [(t, (t + 2) % 8) for t in range(8)])  17.9 us
    ppermute x6, starting transfers between devices, to_left(): return lax.ppermute(a, 'tensor', [(t, (t + 6) % 8) for t in range(8)])  13.3 us
    ppermute x4, waiting for transfers between devices, to_z(): return lax.ppermute(a, 'fsdp', [(0, 1), (1, 0)])  9.07 us
    ppermute x7, starting transfers between devices, to_core(): return lax.ppermute(a, 'tensor', [(t, t ^ 1) for t in range(8)])  6.9 us
    pallas_call x1, Pallas kernels, prepare(): pl.pallas_call(prepare_kernel, out_shape=[sds((QUARTER, 256), BF)] * 2 +...  6.81 us
    ppermute x4, starting transfers between devices, to_z(): return lax.ppermute(a, 'fsdp', [(0, 1), (1, 0)])  6.07 us
    pallas_call x2, Pallas kernels, weight_terms(): pl.pallas_call(dw_kernel, out_shape=[sds((CH, 256), F32), sds((CH, 256),...  5.46 us
    pallas_call x1, Pallas kernels, momentum_step(): pl.pallas_call(momentum_kernel, out_shape=[full, full], grid_spec=pltpu.P...  5.42 us
  transfers between devices with their start and end apart: 27, of which 10 were waited for; matrix products, arithmetic and copies ran while one was open for 1% of the time, Pallas kernels for 29%

commit v1 on v0

--- a/solution.py
+++ b/solution.py
@@ -387,6 +387,59 @@
     )(pre, own, got)
 
 
+def last_moved_kernel(pre, own, got, moved, half):
+    def body(rows):
+        far = pl.ds(pl.multiple_of(rows.start + CH, 128), rows.size)
+        for at, g in ((rows, own), (far, got)):
+            value = pre[at, :] - learn_rate * g[rows, :].astype(F32)
+            moved[at, :] = value.astype(BF)
+            half[at, :] = 0.5 * value
+
+    by_rows(CH, body)
+
+
+def last_moved_chunk(pre, own, got):
+    return pl.pallas_call(
+        last_moved_kernel,
+        out_shape=[sds((2 * CH, 256), BF), sds((2 * CH, 256), F32)],
+        in_specs=[vmem()] * 3,
+        out_specs=[vmem()] * 2,
+        compiler_params=params(12),
+        cost_estimate=cost(0, 7 * MB),
+        name="last_moved_weights",
+    )(pre, own, got)
+
+
+def last_mean_kernel(where, half, partner, *refs):
+    nkw, nvw = refs[-2:]
+
+    def body(rows):
+        mean = half[rows, :] + 0.5 * partner[rows, :].astype(F32)
+        nkw[0, rows, :] = mean[:, :COLS]
+        nvw[0, rows, :] = mean[:, COLS:]
+
+    by_rows(TILE, body)
+
+
+def last_mean(where, half, partner, before):
+    grid, whole, term, moved = chunk_specs(CHUNKS - 1)
+    full = pltpu.HBM((1, HALF, COLS), F32)
+    return pl.pallas_call(
+        last_mean_kernel,
+        out_shape=[full, full],
+        grid_spec=pltpu.PrefetchScalarGridSpec(
+            num_scalar_prefetch=1,
+            grid=grid,
+            in_specs=[moved, moved, anywhere(), anywhere()],
+            out_specs=[whole, whole],
+        ),
+        input_output_aliases={3: 0, 4: 1},
+        compiler_params=params(24),
+        cost_estimate=cost(0, 5 * MB),
+        name="last_average",
+    )(where, half, partner, *before)
+
+
 def momentum_kernel(where, km, vm, *refs):
     own, got, (nkm, nvm) = refs[:CHUNKS], refs[CHUNKS : 2 * CHUNKS], refs[2 * CHUNKS :]
     s, h = pl.program_id(0), pl.program_id(1)
@@ -525,7 +578,8 @@
     o_right = to_right(after(o_relayed, p_send))
     keep, p_send = projection_sum(p_own, to_core(p_send))
     p_z = to_z(p_send)
-    partner1 = to_partner(after(moved_chunk(pre[1], own1, got1), keep), bit)
+    last, half = last_moved_chunk(pre[1], own1, got1)
+    partner1 = to_partner(after(last, keep), bit)
     keys, values = projection_end(where, keep, p_z)
     o_z, o_zc = sum3(o_terms[3], o_right, o_left)
     z, zc = to_z(o_z), to_z_core(o_zc)
@@ -538,7 +592,7 @@
     if bit:
         input_grad = join(where, *parts)
         partner1 = after(partner1, input_grad)
-    weights = mean(where, 1, pre[1], own1, got1, partner1, weights)
+    weights = last_mean(where, half, partner1, weights)
     if not bit:
         input_grad = join(where, *after(parts, weights[0]))
     return keys, values, input_grad, *weights, *momenta

time: 109 us -> 109 us (level)
    pallas_call x0 -> x2, Pallas kernels: none -> 2.42 us  [the longest x1 2.03 us: last_mean(): pl.pallas_call(last_mean_kernel, out_shape=[full, full], grid_spec=pltpu....]
    pallas_call x2 -> x1, Pallas kernels: 4.26 us -> 2.13 us  [mean(): pl.pallas_call(mean_kernel, out_shape=[full, full], grid_spec=pltpu.Prefe...]
  transfers between devices with their start and end apart: 27 -> 27, of which waited for: 10 -> 10; matrix products, arithmetic and copies ran while one was open for 1% -> 1% of each run, Pallas kernels for 29% -> 28%
where the time goes in v1:
time: 109 us
  Pallas kernels  37.1 us (34%)
  starting transfers between devices  34.8 us (32%)
  waiting for transfers between devices  32.7 us (30%)
  between operations  1.46 us (1%)
  other arithmetic  1.21 us (1%)
    ppermute x6, waiting for transfers between devices, to_right(): return lax.ppermute(a, 'tensor', [(t, (t + 2) % 8) for t in range(8)])  18.2 us
    ppermute x6, starting transfers between devices, to_left(): return lax.ppermute(a, 'tensor', [(t, (t + 6) % 8) for t in range(8)])  13.3 us
    ppermute x4, waiting for transfers between devices, to_z(): return lax.ppermute(a, 'fsdp', [(0, 1), (1, 0)])  8.91 us
    ppermute x7, starting transfers between devices, to_core(): return lax.ppermute(a, 'tensor', [(t, t ^ 1) for t in range(8)])  6.8 us
    pallas_call x1, Pallas kernels, prepare(): pl.pallas_call(prepare_kernel, out_shape=[sds((QUARTER, 256), BF)] * 2 +...  6.5 us
    ppermute x4, starting transfers between devices, to_z(): return lax.ppermute(a, 'fsdp', [(0, 1), (1, 0)])  6.08 us
    pallas_call x1, Pallas kernels, momentum_step(): pl.pallas_call(momentum_kernel, out_shape=[full, full], grid_spec=pltpu.P...  5.42 us
    pallas_call x2, Pallas kernels, weight_terms(): pl.pallas_call(dw_kernel, out_shape=[sds((CH, 256), F32), sds((CH, 256),...  5.26 us
  transfers between devices with their start and end apart: 27, of which 10 were waited for; matrix products, arithmetic and copies ran while one was open for 1% of the time, Pallas kernels for 28%

profile of v1, /device:TPU:1, one launch (start us, length us, event | category | flops | bytes accessed | tf_op | source)
XLA Modules:
  0.0 108.5 jit_solution(14057646749481745456)
XLA Ops:
  0.7 1.9 %split_inputs.1 = (bf16[512,256]{1,0:T(8,128)(2,1)S(1)}, bf16[64,2048]{1,0:T(8,128)(2,1)S(1)}, bf16[64,2048]{1,0:T(8,128)(2,1)S(1)}, bf16[64,2048]{1,0:T(8,128)(2,1)S(1)}, bf16[64,2048]{1,0:T(8,128)(2,1)S(1)}) custom-call(s32[3]{0:T(128)S(1)} %pad_add_fusion.where, bf16[64,8192]{1,0:T(8,128)(2,1)} %x.1, bf16[512,128]{1,0:T(8,128)(2,1)} %k.1, bf16[512,128]{1,0:T(8,128)(2,1)} %v.1), custom_call_target="tpu_custom_call" | custom-call | bytes 2600 | tf_op jit(solution)/shard_map/split_inputs/pallas_call | solution.py:87
  6.7 1.6 %collective-permute-start.47 = (bf16[64,2048]{1,0:T(8,128)(2,1)S(1)}, bf16[64,2048]{1,0:T(8,128)(2,1)S(1)}, u32[]{:S(2)}, u32[]{:S(2)}) collective-permute-start(bf16[64,2048]{1,0:T(8,128)(2,1)S(1)} %get-tuple-element.347), channel_id=1, source_target_pairs={{0,8},{8,0},{1,9},{9,1},{2,10},{10,2},{3,11},{11,3},{4,12},{12,4},... | collective-permute-start | bytes 786440 | tf_op jit(solution)/shard_map/ppermute | solution.py:551
  10.3 6.5 %prepare_weights.1 = (bf16[2048,256]{1,0:T(8,128)(2,1)S(1)}, bf16[2048,256]{1,0:T(8,128)(2,1)S(1)}, f32[2048,256]{1,0:T(8,128)}, f32[2048,256]{1,0:T(8,128)}) custom-call(s32[3]{0:T(128)S(1)} %pad_add_fusion.where, f32[1,4096,128]{2,1,0:T(8,128)} %kw.1, f32[1,4096,128]{2,1,0:T(8,128)} %vw.1, f32[1,4096,128]{2,1,0:T(8,128)} %km.1, f32[1,4096,128]{2,1,0:T(8,128)} %vm.1), custom_call_target="tpu_custom_call" | custom-call | bytes 14680 | tf_op jit(solution)/shard_map/prepare_weights/pallas_call | solution.py:132
  16.8 4.0 %collective-permute-done.48 = bf16[64,2048]{1,0:T(8,128)(2,1)S(1)} collective-permute-done((bf16[64,2048]{1,0:T(8,128)(2,1)S(1)}, bf16[64,2048]{1,0:T(8,128)(2,1)S(1)}, u32[]{:S(2)}, u32[]{:S(2)}) %collective-permute-start.48) | collective-permute-done | bytes 262176 | tf_op jit(solution)/shard_map/ppermute | solution.py:555
  25.8 5.7 %collective-permute-done.55 = bf16[512,256]{1,0:T(8,128)(2,1)S(1)} collective-permute-done((bf16[512,256]{1,0:T(8,128)(2,1)S(1)}, bf16[512,256]{1,0:T(8,128)(2,1)S(1)}, u32[]{:S(2)}, u32[]{:S(2)}) %collective-permute-start.55) | collective-permute-done | bytes 262176 | tf_op jit(solution)/shard_map/ppermute | solution.py:551
  31.6 5.1 %collective-permute-done.51 = bf16[128,2048]{1,0:T(8,128)(2,1)S(1)} collective-permute-done((bf16[128,2048]{1,0:T(8,128)(2,1)S(1)}, bf16[128,2048]{1,0:T(8,128)(2,1)S(1)}, u32[]{:S(2)}, u32[]{:S(2)}) %collective-permute-start.51) | collective-permute-done | bytes 524320 | tf_op jit(solution)/shard_map/ppermute | solution.py:539
  38.2 2.6 %collective-permute-start.52 = (bf16[128,2048]{1,0:T(8,128)(2,1)}, bf16[128,2048]{1,0:T(8,128)(2,1)}, u32[]{:S(2)}, u32[]{:S(2)}) collective-permute-start(bf16[128,2048]{1,0:T(8,128)(2,1)} %collective-permute-done.50), channel_id=1, source_target_pairs={{0,6},{1,7},{2,0},{3,1},{4,2},{5,3},{6,4},{7,5},{8,14},{9,15},{10,... | collective-permute-start | bytes 1572872 | tf_op jit(solution)/shard_map/ppermute | solution.py:543
  42.1 4.1 %input_terms.1 = (bf16[128,2048]{1,0:T(8,128)(2,1)S(1)}, bf16[128,2048]{1,0:T(8,128)(2,1)S(1)}, bf16[128,2048]{1,0:T(8,128)(2,1)S(1)}, bf16[128,2048]{1,0:T(8,12...) custom-call(bf16[1024,512]{1,0:T(8,128)(2,1)S(1)} %order_cotangents., ...), custom_call_target="tpu_custom_call" | custom-call | flops 2147483 | bytes 7340 | tf_op jit(solution)/shard_map/input_terms/pallas_call | solution.py:193
  46.2 6.9 %collective-permute-done.53 = bf16[128,2048]{1,0:T(8,128)(2,1)} collective-permute-done((bf16[128,2048]{1,0:T(8,128)(2,1)}, bf16[128,2048]{1,0:T(8,128)(2,1)}, u32[]{:S(2)}, u32[]{:S(2)}) %collective-permute-start.53) | collective-permute-done | bytes 524320 | tf_op jit(solution)/shard_map/ppermute | solution.py:539
  53.2 55.3 %conditional.1 = (bf16[512,128]{1,0:T(8,128)(2,1)}, bf16[512,128]{1,0:T(8,128)(2,1)}, f32[1,4096,128]{2,1,0:T(8,128)}, f32[1,4096,128]{2,1,0:T(8,128)}, f32[1,40...) conditional(s32[]{:T(128)} %clamp.3, ...), branch_computations={%region_0.1_spmd, %region_1.2_spmd, %region_2.3_spmd} | conditional | flops 4819253 | bytes 43058352 | solution.py:627
  53.4 2.6 %weight_terms.8 = (f32[1024,256]{1,0:T(8,128)S(1)}, bf16[1024,256]{1,0:T(8,128)(2,1)S(1)}) custom-call(bf16[1024,512]{1,0:T(8,128)(2,1)S(1)} %get-tuple-element.231.kv, bf16[128,2048]{1,0:T(8,128)(2,1)S(1)} %get-tuple-element.203.refs_0_, bf16[128,2048]{1,0:T(8,128)(2,1)} %get-tuple-element.204.refs_1_, bf16[128,2048]{1,0:T(8,128)(2,1)S(1)} %get-tuple-element.205.refs_2_, ...), custom_call_target="tpu_custom_call" | custom-call | flops 1073741 | bytes 5242 | tf_op jit(solution)/shard_map/cond/branch_1_fun/weight_terms/pallas_call | solution.py:216
  56.9 2.7 %collective-permute-start.19 = (bf16[128,2048]{1,0:T(8,128)(2,1)S(1)}, bf16[128,2048]{1,0:T(8,128)(2,1)S(1)}, u32[]{:S(2)}, u32[]{:S(2)}) collective-permute-start(bf16[128,2048]{1,0:T(8,128)(2,1)S(1)} %get-tuple-element.224), channel_id=1, source_target_pairs={{0,6},{1,7},{2,0},{3,1},{4,2},{5,3},{6,4},{7,5},{8,14},{9,15},{10,... | collective-permute-start | bytes 1572872 | tf_op jit(solution)/shard_map/cond/branch_1_fun/ppermute | solution.py:543
  61.2 5.1 %projection.4 = (f32[1024,256]{1,0:T(8,128)S(1)}, bf16[1024,256]{1,0:T(8,128)(2,1)S(1)}) custom-call(bf16[128,2048]{1,0:T(8,128)(2,1)S(1)} %get-tuple-element.203.refs_0_, bf16[128,2048]{1,0:T(8,128)(2,1)} %get-tuple-element.204.refs_1_, bf16[128,2048]{1,0:T(8,128)(2,1)S(1)} %get-tuple-element.205.refs_2_, bf16[128,2048]{1,0:T(8,128)(2,1)} %get-tuple-element.206.refs_3_, ...), custom_call_target="tpu_custom_call" | custom-call | flops 2147483 | bytes 8388 | tf_op jit(solution)/shard_map/cond/branch_1_fun/projection/pallas_call | solution.py:251
  67.2 2.6 %weight_terms.9 = (f32[1024,256]{1,0:T(8,128)S(1)}, bf16[1024,256]{1,0:T(8,128)(2,1)S(1)}) custom-call(bf16[1024,512]{1,0:T(8,128)(2,1)S(1)} %get-tuple-element.231.kv, bf16[128,2048]{1,0:T(8,128)(2,1)S(1)} %get-tuple-element.203.refs_0_, bf16[128,2048]{1,0:T(8,128)(2,1)} %get-tuple-element.204.refs_1_, bf16[128,2048]{1,0:T(8,128)(2,1)S(1)} %get-tuple-element.205.refs_2_, ...), custom_call_target="tpu_custom_call" | custom-call | flops 1073741 | bytes 5242 | tf_op jit(solution)/shard_map/cond/branch_1_fun/weight_terms/pallas_call | solution.py:216
  70.0 1.6 %collective-permute-done.17 = bf16[128,2048]{1,0:T(8,128)(2,1)S(1)} collective-permute-done((bf16[128,2048]{1,0:T(8,128)(2,1)S(1)}, bf16[128,2048]{1,0:T(8,128)(2,1)S(1)}, u32[]{:S(2)}, u32[]{:S(2)}) %collective-permute-start.17) | collective-permute-done | bytes 524320 | tf_op jit(solution)/shard_map/cond/branch_1_fun/ppermute | solution.py:539
  71.8 2.7 %collective-permute-start.24 = (bf16[128,2048]{1,0:T(8,128)(2,1)S(1)}, bf16[128,2048]{1,0:T(8,128)(2,1)S(1)}, u32[]{:S(2)}, u32[]{:S(2)}) collective-permute-start(bf16[128,2048]{1,0:T(8,128)(2,1)S(1)} %get-tuple-element.245), channel_id=1, source_target_pairs={{0,6},{1,7},{2,0},{3,1},{4,2},{5,3},{6,4},{7,5},{8,14},{9,15},{10,... | collective-permute-start | bytes 1572872 | tf_op jit(solution)/shard_map/cond/branch_1_fun/ppermute | solution.py:543
  77.8 3.2 %collective-permute-done.16.got = bf16[512,256]{1,0:T(8,128)(2,1)S(1)} collective-permute-done((bf16[512,256]{1,0:T(8,128)(2,1)S(1)}, bf16[512,256]{1,0:T(8,128)(2,1)S(1)}, u32[]{:S(2)}, u32[]{:S(2)}) %collective-permute-start.16) | collective-permute-done | bytes 262176 | tf_op jit(solution)/shard_map/cond/branch_1_fun/ppermute | solution.py:551
  81.0 4.6 %collective-permute-done.18.b = bf16[128,2048]{1,0:T(8,128)(2,1)S(1)} collective-permute-done((bf16[128,2048]{1,0:T(8,128)(2,1)S(1)}, bf16[128,2048]{1,0:T(8,128)(2,1)S(1)}, u32[]{:S(2)}, u32[]{:S(2)}) %collective-permute-start.18) | collective-permute-done | bytes 524320 | tf_op jit(solution)/shard_map/cond/branch_1_fun/ppermute | solution.py:539
  86.0 2.1 %average.4 = (f32[1,4096,128]{2,1,0:T(8,128)}, f32[1,4096,128]{2,1,0:T(8,128)}) custom-call(s32[3]{0:T(128)S(1)} %get-tuple-element.226.where, f32[2048,256]{1,0:T(8,128)S(1)} %get-tuple-element.237.pre, f32[1024,256]{1,0:T(8,128)S(1)} %get-tuple-element.230.refs_0_.own, bf16[1024,256]{1,0:T(8,128)(2,1)S(1)} %collective-permute-done.20.refs_2_.got, ...), custom_call_target="tpu_custom_call" | custom-call | bytes 8388 | tf_op jit(solution)/shard_map/cond/branch_1_fun/average/pallas_call | solution.py:522
  88.1 2.7 %collective-permute-start.25 = (bf16[128,2048]{1,0:T(8,128)(2,1)S(1)}, bf16[128,2048]{1,0:T(8,128)(2,1)S(1)}, u32[]{:S(2)}, u32[]{:S(2)}) collective-permute-start(bf16[128,2048]{1,0:T(8,128)(2,1)S(1)} %add.21), channel_id=1, source_target_pairs={{0,6},{1,7},{2,0},{3,1},{4,2},{5,3},{6,4},{7,5},{8,14},{9,15},{10,... | collective-permute-start | bytes 1572872 | tf_op jit(solution)/shard_map/cond/branch_1_fun/ppermute | solution.py:543
  92.2 2.5 %collective-permute-start.28 = (bf16[64,2048]{1,0:T(8,128)(2,1)S(1)}, bf16[64,2048]{1,0:T(8,128)(2,1)S(1)}, u32[]{:S(2)}, u32[]{:S(2)}) collective-permute-start(bf16[64,2048]{1,0:T(8,128)(2,1)S(1)} %get-tuple-element.249), channel_id=1, source_target_pairs={{0,9},{1,8},{2,11},{3,10},{4,13},{5,12},{6,15},{7,14},{8,1},{9,0},... | collective-permute-start | bytes 786440 | tf_op jit(solution)/shard_map/cond/branch_1_fun/ppermute | solution.py:555
  94.7 5.4 %momentum_step.4 = (f32[1,4096,128]{2,1,0:T(8,128)}, f32[1,4096,128]{2,1,0:T(8,128)}) custom-call(s32[3]{0:T(128)S(1)} %get-tuple-element.226.where, f32[1,4096,128]{2,1,0:T(8,128)} %get-tuple-element.227.km, f32[1,4096,128]{2,1,0:T(8,128)} %get-tuple-element.228.vm, f32[1024,256]{1,0:T(8,128)S(1)} %get-tuple-element.230.refs_0_.own, ...), custom_call_target="tpu_custom_call" | custom-call | bytes 11534 | tf_op jit(solution)/shard_map/cond/branch_1_fun/momentum_step/pallas_call | solution.py:482
  100.4 2.8 %collective-permute-start.26 = (bf16[64,2048]{1,0:T(8,128)(2,1)S(1)}, bf16[64,2048]{1,0:T(8,128)(2,1)S(1)}, u32[]{:S(2)}, u32[]{:S(2)}) collective-permute-start(bf16[64,2048]{1,0:T(8,128)(2,1)S(1)} %get-tuple-element.248), channel_id=1, source_target_pairs={{0,1},{1,0},{2,3},{3,2},{4,5},{5,4},{6,7},{7,6},{8,9},{9,8},{10,11... | collective-permute-start | bytes 786440 | tf_op jit(solution)/shard_map/cond/branch_1_fun/ppermute | solution.py:547
  106.5 2.0 %last_average.4 = (f32[1,4096,128]{2,1,0:T(8,128)}, f32[1,4096,128]{2,1,0:T(8,128)}) custom-call(s32[3]{0:T(128)S(1)} %get-tuple-element.226.where, f32[2048,256]{1,0:T(8,128)S(1)} %get-tuple-element.251.half, bf16[2048,256]{1,0:T(8,128)(2,1)S(1)} %collective-permute-done.29.partner, ...), custom_call_target="tpu_custom_call", output_to_operand_aliasing={{0}: (3, {}), {1}: (4, {})} | custom-call | bytes 5242 | tf_op jit(solution)/shard_map/cond/branch_1_fun/last_average/pallas_call | solution.py:427
  (75 shorter events, 25.6 us)
Async XLA Ops:
  5.3 16.4 %collective-permute-start.46 = (bf16[128,2048]{1,0:T(8,128)(2,1)S(1)}, bf16[128,2048]{1,0:T(8,128)(2,1)S(1)}, u32[]{:S(2)}, u32[]{:S(2)}) collective-permute-start(bf16[128,2048]{1,0:T(8,128)(2,1)S(1)} %constant_dynamic-update-slice_fusion), channel_id=1, source_target_pairs={{0,2},{1,3},{2,4},{3,5},{4,6},{5,7},{6,0},{7,1},{8,10},{9,11},{10,... | collective-permute-start | bytes 1572872 | tf_op jit(solution)/shard_map/ppermute | solution.py:539
  6.7 10.1 %collective-permute-start.47 = (bf16[64,2048]{1,0:T(8,128)(2,1)S(1)}, bf16[64,2048]{1,0:T(8,128)(2,1)S(1)}, u32[]{:S(2)}, u32[]{:S(2)}) collective-permute-start(bf16[64,2048]{1,0:T(8,128)(2,1)S(1)} %get-tuple-element.347), channel_id=1, source_target_pairs={{0,8},{8,0},{1,9},{9,1},{2,10},{10,2},{3,11},{11,3},{4,12},{12,4},... | collective-permute-start | bytes 786440 | tf_op jit(solution)/shard_map/ppermute | solution.py:551
  8.4 12.5 %collective-permute-start.48 = (bf16[64,2048]{1,0:T(8,128)(2,1)S(1)}, bf16[64,2048]{1,0:T(8,128)(2,1)S(1)}, u32[]{:S(2)}, u32[]{:S(2)}) collective-permute-start(bf16[64,2048]{1,0:T(8,128)(2,1)S(1)} %get-tuple-element.348), channel_id=1, source_target_pairs={{0,9},{1,8},{2,11},{3,10},{4,13},{5,12},{6,15},{7,14},{8,1},{9,0},... | collective-permute-start | bytes 786440 | tf_op jit(solution)/shard_map/ppermute | solution.py:555
  9.0 15.4 %collective-permute-start.49 = (bf16[128,2048]{1,0:T(8,128)(2,1)S(1)}, bf16[128,2048]{1,0:T(8,128)(2,1)S(1)}, u32[]{:S(2)}, u32[]{:S(2)}) collective-permute-start(bf16[128,2048]{1,0:T(8,128)(2,1)S(1)} %constant_dynamic-update-slice_fusion), channel_id=1, source_target_pairs={{0,6},{1,7},{2,0},{3,1},{4,2},{5,3},{6,4},{7,5},{8,14},{9,15},{10,... | collective-permute-start | bytes 1572872 | tf_op jit(solution)/shard_map/ppermute | solution.py:543
  21.7 15.0 %collective-permute-start.51 = (bf16[128,2048]{1,0:T(8,128)(2,1)S(1)}, bf16[128,2048]{1,0:T(8,128)(2,1)S(1)}, u32[]{:S(2)}, u32[]{:S(2)}) collective-permute-start(bf16[128,2048]{1,0:T(8,128)(2,1)S(1)} %collective-permute-done.46), channel_id=1, source_target_pairs={{0,2},{1,3},{2,4},{3,5},{4,6},{5,7},{6,0},{7,1},{8,10},{9,11},{10,... | collective-permute-start | bytes 1572872 | tf_op jit(solution)/shard_map/ppermute | solution.py:539
  23.0 19.1 %collective-permute-start.54 = (bf16[2048,256]{1,0:T(8,128)(2,1)S(1)}, bf16[2048,256]{1,0:T(8,128)(2,1)}, u32[]{:S(2)}, u32[]{:S(2)}) collective-permute-start(bf16[2048,256]{1,0:T(8,128)(2,1)S(1)} %get-tuple-element.357), channel_id=1, source_target_pairs={{0,1},{1,0},{2,3},{3,2},{4,5},{5,4},{6,7},{7,6},{8,9},{9,8},{10,11... | collective-permute-start | bytes 3145736 | tf_op jit(solution)/shard_map/ppermute | solution.py:547
  23.0 15.2 %collective-permute-start.50 = (bf16[128,2048]{1,0:T(8,128)(2,1)}, bf16[128,2048]{1,0:T(8,128)(2,1)}, u32[]{:S(2)}, u32[]{:S(2)}) collective-permute-start(bf16[128,2048]{1,0:T(8,128)(2,1)} %pad_maximum_fusion), channel_id=1, source_target_pairs={{0,6},{1,7},{2,0},{3,1},{4,2},{5,3},{6,4},{7,5},{8,14},{9,15},{10,... | collective-permute-start | bytes 1572872 | tf_op jit(solution)/shard_map/ppermute | solution.py:543
  24.4 7.1 %collective-permute-start.55 = (bf16[512,256]{1,0:T(8,128)(2,1)S(1)}, bf16[512,256]{1,0:T(8,128)(2,1)S(1)}, u32[]{:S(2)}, u32[]{:S(2)}) collective-permute-start(bf16[512,256]{1,0:T(8,128)(2,1)S(1)} %get-tuple-element.358), channel_id=1, source_target_pairs={{0,8},{8,0},{1,9},{9,1},{2,10},{10,2},{3,11},{11,3},{4,12},{12,4},... | collective-permute-start | bytes 786440 | tf_op jit(solution)/shard_map/ppermute | solution.py:551
  38.0 15.1 %collective-permute-start.53 = (bf16[128,2048]{1,0:T(8,128)(2,1)}, bf16[128,2048]{1,0:T(8,128)(2,1)}, u32[]{:S(2)}, u32[]{:S(2)}) collective-permute-start(bf16[128,2048]{1,0:T(8,128)(2,1)} %pad_maximum_fusion), channel_id=1, source_target_pairs={{0,2},{1,3},{2,4},{3,5},{4,6},{5,7},{6,0},{7,1},{8,10},{9,11},{10,... | collective-permute-start | bytes 1572872 | tf_op jit(solution)/shard_map/ppermute | solution.py:539
  38.2 15.0 %collective-permute-start.52 = (bf16[128,2048]{1,0:T(8,128)(2,1)}, bf16[128,2048]{1,0:T(8,128)(2,1)}, u32[]{:S(2)}, u32[]{:S(2)}) collective-permute-start(bf16[128,2048]{1,0:T(8,128)(2,1)} %collective-permute-done.50), channel_id=1, source_target_pairs={{0,6},{1,7},{2,0},{3,1},{4,2},{5,3},{6,4},{7,5},{8,14},{9,15},{10,... | collective-permute-start | bytes 1572872 | tf_op jit(solution)/shard_map/ppermute | solution.py:543
  56.9 14.7 %collective-permute-start.17 = (bf16[128,2048]{1,0:T(8,128)(2,1)S(1)}, bf16[128,2048]{1,0:T(8,128)(2,1)S(1)}, u32[]{:S(2)}, u32[]{:S(2)}) collective-permute-start(bf16[128,2048]{1,0:T(8,128)(2,1)S(1)} %get-tuple-element.222), channel_id=1, source_target_pairs={{0,2},{1,3},{2,4},{3,5},{4,6},{5,7},{6,0},{7,1},{8,10},{9,11},{10,... | collective-permute-start | bytes 1572872 | tf_op jit(solution)/shard_map/cond/branch_1_fun/ppermute | solution.py:539
  56.9 14.9 %collective-permute-start.19 = (bf16[128,2048]{1,0:T(8,128)(2,1)S(1)}, bf16[128,2048]{1,0:T(8,128)(2,1)S(1)}, u32[]{:S(2)}, u32[]{:S(2)}) collective-permute-start(bf16[128,2048]{1,0:T(8,128)(2,1)S(1)} %get-tuple-element.224), channel_id=1, source_target_pairs={{0,6},{1,7},{2,0},{3,1},{4,2},{5,3},{6,4},{7,5},{8,14},{9,15},{10,... | collective-permute-start | bytes 1572872 | tf_op jit(solution)/shard_map/cond/branch_1_fun/ppermute | solution.py:543
  59.9 26.1 %collective-permute-start.22 = (bf16[2048,256]{1,0:T(8,128)(2,1)S(1)}, bf16[2048,256]{1,0:T(8,128)(2,1)S(1)}, u32[]{:S(2)}, u32[]{:S(2)}) collective-permute-start(bf16[2048,256]{1,0:T(8,128)(2,1)S(1)} %moved_weights.4), channel_id=1, source_target_pairs={{0,32},{16,48},{32,0},{48,16},{64,96},{80,112},{96,64},{112,80},{1... | collective-permute-start | bytes 3145736 | tf_op jit(solution)/shard_map/cond/branch_1_fun/ppermute | solution.py:560
  66.3 8.2 %collective-permute-start.15 = (bf16[1024,256]{1,0:T(8,128)(2,1)S(1)}, bf16[1024,256]{1,0:T(8,128)(2,1)S(1)}, u32[]{:S(2)}, u32[]{:S(2)}) collective-permute-start(bf16[1024,256]{1,0:T(8,128)(2,1)S(1)} %get-tuple-element.214), channel_id=1, source_target_pairs={{0,1},{1,0},{2,3},{3,2},{4,5},{5,4},{6,7},{7,6},{8,9},{9,8},{10,11... | collective-permute-start | bytes 1572872 | tf_op jit(solution)/shard_map/cond/branch_1_fun/ppermute | solution.py:547
  69.9 6.2 %collective-permute-start.21 = (bf16[1024,256]{1,0:T(8,128)(2,1)S(1)}, bf16[1024,256]{1,0:T(8,128)(2,1)S(1)}, u32[]{:S(2)}, u32[]{:S(2)}) collective-permute-start(bf16[1024,256]{1,0:T(8,128)(2,1)S(1)} %get-tuple-element.234), channel_id=1, source_target_pairs={{0,1},{1,0},{2,3},{3,2},{4,5},{5,4},{6,7},{7,6},{8,9},{9,8},{10,11... | collective-permute-start | bytes 1572872 | tf_op jit(solution)/shard_map/cond/branch_1_fun/ppermute | solution.py:547
  71.7 13.9 %collective-permute-start.18 = (bf16[128,2048]{1,0:T(8,128)(2,1)S(1)}, bf16[128,2048]{1,0:T(8,128)(2,1)S(1)}, u32[]{:S(2)}, u32[]{:S(2)}) collective-permute-start(bf16[128,2048]{1,0:T(8,128)(2,1)S(1)} %add.20), channel_id=1, source_target_pairs={{0,2},{1,3},{2,4},{3,5},{4,6},{5,7},{6,0},{7,1},{8,10},{9,11},{10,... | collective-permute-start | bytes 1572872 | tf_op jit(solution)/shard_map/cond/branch_1_fun/ppermute | solution.py:539
  71.8 14.0 %collective-permute-start.24 = (bf16[128,2048]{1,0:T(8,128)(2,1)S(1)}, bf16[128,2048]{1,0:T(8,128)(2,1)S(1)}, u32[]{:S(2)}, u32[]{:S(2)}) collective-permute-start(bf16[128,2048]{1,0:T(8,128)(2,1)S(1)} %get-tuple-element.245), channel_id=1, source_target_pairs={{0,6},{1,7},{2,0},{3,1},{4,2},{5,3},{6,4},{7,5},{8,14},{9,15},{10,... | collective-permute-start | bytes 1572872 | tf_op jit(solution)/shard_map/cond/branch_1_fun/ppermute | solution.py:543
  74.6 6.5 %collective-permute-start.16 = (bf16[512,256]{1,0:T(8,128)(2,1)S(1)}, bf16[512,256]{1,0:T(8,128)(2,1)S(1)}, u32[]{:S(2)}, u32[]{:S(2)}) collective-permute-start(bf16[512,256]{1,0:T(8,128)(2,1)S(1)} %get-tuple-element.216), channel_id=1, source_target_pairs={{0,8},{8,0},{1,9},{9,1},{2,10},{10,2},{3,11},{11,3},{4,12},{12,4},... | collective-permute-start | bytes 786440 | tf_op jit(solution)/shard_map/cond/branch_1_fun/ppermute | solution.py:551
  76.5 30.0 %collective-permute-start.29 = (bf16[2048,256]{1,0:T(8,128)(2,1)S(1)}, bf16[2048,256]{1,0:T(8,128)(2,1)S(1)}, u32[]{:S(2)}, u32[]{:S(2)}) collective-permute-start(bf16[2048,256]{1,0:T(8,128)(2,1)S(1)} %get-tuple-element.253), channel_id=1, source_target_pairs={{0,32},{16,48},{32,0},{48,16},{64,96},{80,112},{96,64},{112,80},{1... | collective-permute-start | bytes 3145736 | tf_op jit(solution)/shard_map/cond/branch_1_fun/ppermute | solution.py:560
  85.6 14.6 %collective-permute-start.23 = (bf16[128,2048]{1,0:T(8,128)(2,1)S(1)}, bf16[128,2048]{1,0:T(8,128)(2,1)S(1)}, u32[]{:S(2)}, u32[]{:S(2)}) collective-permute-start(bf16[128,2048]{1,0:T(8,128)(2,1)S(1)} %get-tuple-element.242), channel_id=1, source_target_pairs={{0,2},{1,3},{2,4},{3,5},{4,6},{5,7},{6,0},{7,1},{8,10},{9,11},{10,... | collective-permute-start | bytes 1572872 | tf_op jit(solution)/shard_map/cond/branch_1_fun/ppermute | solution.py:539
  88.1 12.1 %collective-permute-start.25 = (bf16[128,2048]{1,0:T(8,128)(2,1)S(1)}, bf16[128,2048]{1,0:T(8,128)(2,1)S(1)}, u32[]{:S(2)}, u32[]{:S(2)}) collective-permute-start(bf16[128,2048]{1,0:T(8,128)(2,1)S(1)} %add.21), channel_id=1, source_target_pairs={{0,6},{1,7},{2,0},{3,1},{4,2},{5,3},{6,4},{7,5},{8,14},{9,15},{10,... | collective-permute-start | bytes 1572872 | tf_op jit(solution)/shard_map/cond/branch_1_fun/ppermute | solution.py:543
  90.8 13.9 %collective-permute-start.27 = (bf16[64,2048]{1,0:T(8,128)(2,1)S(1)}, bf16[64,2048]{1,0:T(8,128)(2,1)S(1)}, u32[]{:S(2)}, u32[]{:S(2)}) collective-permute-start(bf16[64,2048]{1,0:T(8,128)(2,1)S(1)} %get-tuple-element.225), channel_id=1, source_target_pairs={{0,8},{8,0},{1,9},{9,1},{2,10},{10,2},{3,11},{11,3},{4,12},{12,4},... | collective-permute-start | bytes 786440 | tf_op jit(solution)/shard_map/cond/branch_1_fun/ppermute | solution.py:551
  92.2 12.5 %collective-permute-start.28 = (bf16[64,2048]{1,0:T(8,128)(2,1)S(1)}, bf16[64,2048]{1,0:T(8,128)(2,1)S(1)}, u32[]{:S(2)}, u32[]{:S(2)}) collective-permute-start(bf16[64,2048]{1,0:T(8,128)(2,1)S(1)} %get-tuple-element.249), channel_id=1, source_target_pairs={{0,9},{1,8},{2,11},{3,10},{4,13},{5,12},{6,15},{7,14},{8,1},{9,0},... | collective-permute-start | bytes 786440 | tf_op jit(solution)/shard_map/cond/branch_1_fun/ppermute | solution.py:555
  100.4 4.3 %collective-permute-start.26 = (bf16[64,2048]{1,0:T(8,128)(2,1)S(1)}, bf16[64,2048]{1,0:T(8,128)(2,1)S(1)}, u32[]{:S(2)}, u32[]{:S(2)}) collective-permute-start(bf16[64,2048]{1,0:T(8,128)(2,1)S(1)} %get-tuple-element.248), channel_id=1, source_target_pairs={{0,1},{1,0},{2,3},{3,2},{4,5},{5,4},{6,7},{7,6},{8,9},{9,8},{10,11... | collective-permute-start | bytes 786440 | tf_op jit(solution)/shard_map/cond/branch_1_fun/ppermute | solution.py:547
  (13 other events, 113.5 us)
